TPU v7x, 256 devices: a whole 4x4x8 slice. The times are simulated.
256 devices in a mesh: dp: 4 (over x), expert: 8 (over z), etp: 8 (over y, core).
Axes of the slice: x: 4, y: 4, z: 8, core: 2. Of those that a mesh axis runs over, the one named last changes fastest.
Arguments:
- grad_output: bfloat16 [2048, 6144], P(('dp', 'expert', 'etp')), may hold values from -6 to 6
- comb_weights: bfloat16 [2048, 4], P(('dp', 'expert', 'etp')), may hold values from 0.099609375 to 1
- expert_ids: int32 [2048, 4], P(('dp', 'expert', 'etp')), may hold values from 0 to 7, all different within a row; in each aligned block of 8 rows (0 to 7, 8 to 15, ...) at most 6 rows name the same one
- down_weight: bfloat16 [8, 6144, 6144], P('expert', 'etp', 'dp'), may hold values from -0.078125 to 0.078125
- gate_weight: bfloat16 [8, 6144, 6144], P('expert', 'dp', 'etp'), may hold values from -0.078125 to 0.078125
- up_weight: bfloat16 [8, 6144, 6144], P('expert', 'dp', 'etp'), may hold values from -0.078125 to 0.078125
- gate_saved: bfloat16 [8, 1536, 6144], P('expert', None, 'etp'), may hold values from -6 to 6
- up_saved: bfloat16 [8, 1536, 6144], P('expert', None, 'etp'), may hold values from -6 to 6
Outputs:
- input_grad: bfloat16 [2048, 6144], P(('dp', 'expert', 'etp'))
Inputs may be any that keep to these rules, and one draw needn't show every extreme that they name: `expert_ids`: each token names 4 different experts; no expert is named by more than 6 of the tokens of one device.
All inputs are finite; a program needn't handle non-finite values.
Results may differ from a plain program's by a relative error of at most 0.0049.
Values may be sent and summed in bfloat16 or wider, within the bound.
A program may use at most 128 MiB of HBM per device.

v0:
```python
import jax
import jax.numpy as jnp
from jax import lax
from jax.sharding import PartitionSpec as P


def swiglu_backward(hidden_raw, weight, gate_pre, up_pre):
    gate_value = gate_pre.astype(jnp.float32)
    up_value = up_pre.astype(jnp.float32)
    sigmoid_gate = jax.nn.sigmoid(gate_value)
    scaled = hidden_raw * weight[:, None]
    gate_grad = (
        scaled * up_value * sigmoid_gate * (1.0 + gate_value * (1.0 - sigmoid_gate))
    ).astype(jnp.bfloat16)
    up_grad = (scaled * gate_value * sigmoid_gate).astype(jnp.bfloat16)
    return (gate_grad, up_grad)


def on_device(
    grad_output, comb_weights, expert_ids, down_weight, gate_weight, up_weight, gate_saved, up_saved
):
    group_count = lax.axis_size("dp")
    expert_count = lax.axis_size("expert")
    tensor_count = lax.axis_size("etp")
    tokens_here, model_width = grad_output.shape
    choices_count = expert_ids.shape[1]
    capacity = min(
        tokens_here, tokens_here * choices_count // expert_count + max(2, tokens_here // 6)
    )
    quarter = model_width // group_count
    labels = jnp.arange(expert_count, dtype=jnp.int32)
    matches = (expert_ids[:, :, None] == labels[None, None, :]).astype(jnp.int32)
    expert_hits = jnp.sum(matches, axis=1)
    before = jnp.cumsum(expert_hits, axis=0) - expert_hits
    position = jnp.sum(matches * before[:, None, :], axis=2)
    target = expert_ids * capacity + position
    slot_labels = jnp.arange(expert_count * capacity, dtype=jnp.int32)
    chosen = slot_labels[:, None, None] == target[None, :, :]
    selector = (
        jnp.any(chosen, axis=2).astype(jnp.bfloat16).reshape(expert_count, capacity, tokens_here)
    )
    pieces = grad_output.reshape(tokens_here, group_count, quarter)
    outgoing = jnp.einsum(
        "ect,tqd->eqcd", selector, pieces, preferred_element_type=jnp.float32
    ).astype(jnp.bfloat16)
    weight_slots = jnp.sum(
        jnp.where(chosen, comb_weights.astype(jnp.float32)[None, :, :], 0.0), axis=(1, 2)
    )
    weight_out = jnp.broadcast_to(
        weight_slots.reshape(expert_count, 1, capacity), (expert_count, group_count, capacity)
    ).astype(jnp.bfloat16)
    arrived, arrived_weight = (
        lax.all_to_all(outgoing, "dp", split_axis=1, concat_axis=1, tiled=True),
        lax.all_to_all(weight_out, "dp", split_axis=1, concat_axis=1, tiled=True),
    )
    copied = jnp.broadcast_to(
        arrived[:, None], (expert_count, tensor_count, group_count, capacity, quarter)
    )
    copied = copied.reshape(expert_count * tensor_count, group_count, capacity, quarter)
    copied_weight = jnp.broadcast_to(
        arrived_weight[:, None], (expert_count, tensor_count, group_count, capacity)
    )
    copied_weight = copied_weight.reshape(expert_count * tensor_count, group_count, capacity)
    routed, routed_weight = (
        lax.all_to_all(copied, ("expert", "etp"), split_axis=0, concat_axis=0, tiled=True),
        lax.all_to_all(copied_weight, ("expert", "etp"), split_axis=0, concat_axis=0, tiled=True),
    )
    slot_total = expert_count * tensor_count * group_count * capacity
    routed = routed.reshape(slot_total, quarter)
    slot_weight = routed_weight.reshape(slot_total).astype(jnp.float32)
    down_local = down_weight[0]
    gate_local = gate_saved[0]
    up_local = up_saved[0]
    partial_value = jnp.einsum("sq,fq->sf", routed, down_local, preferred_element_type=jnp.float32)
    hidden_raw = lax.psum(partial_value, "dp")
    gate_grad, up_grad = swiglu_backward(hidden_raw, slot_weight, gate_local, up_local)
    slot_grad = jnp.einsum(
        "sf,qf->sq", gate_grad, gate_weight[0], preferred_element_type=jnp.float32
    )
    slot_grad = slot_grad + jnp.einsum(
        "sf,qf->sq", up_grad, up_weight[0], preferred_element_type=jnp.float32
    )
    outbound = slot_grad.reshape(expert_count * tensor_count, group_count, capacity, quarter)
    inbound = lax.all_to_all(outbound, ("expert", "etp"), split_axis=0, concat_axis=0, tiled=True)
    inbound = jnp.sum(
        inbound.reshape(expert_count, tensor_count, group_count, capacity, quarter), axis=1
    )
    complete = lax.all_to_all(inbound, "dp", split_axis=1, concat_axis=3, tiled=True)
    complete = complete.reshape(expert_count * capacity, model_width)
    picked = jnp.take(complete, target.reshape(-1), axis=0)
    picked = picked.reshape(tokens_here, choices_count, model_width)
    return jnp.sum(picked, axis=1).astype(jnp.bfloat16)


def solution(mesh):
    in_specs = (
        P(("dp", "expert", "etp"), None),
        P(("dp", "expert", "etp"), None),
        P(("dp", "expert", "etp"), None),
        P("expert", "etp", "dp"),
        P("expert", "dp", "etp"),
        P("expert", "dp", "etp"),
        P("expert", None, "etp"),
        P("expert", None, "etp"),
    )
    out_specs = P(("dp", "expert", "etp"), None)
    return jax.shard_map(
        on_device, mesh=mesh, in_specs=in_specs, out_specs=out_specs, check_vma=False
    )
```

profile of v0, /device:TPU:32, one launch (start us, length us, event | category | flops | bytes accessed | tf_op | source)
XLA Modules:
  0.0 574.1 jit_solution(5975261550007912184)
XLA Ops:
  6.5 0.0 copy-start
  6.5 0.0 all-reduce.2.cloned.1.call-start
  6.5 0.9 convert_reduce_fusion
  7.5 0.9 select_reduce_fusion.2
  8.4 0.7 compare_and_fusion
  9.1 0.1 fusion.22
  9.2 0.1 reshape.97
  9.2 0.1 copy.61
  9.4 1.2 fusion.9
  10.6 14.3 %all_to_all.40 = bf16[8,4,6,1536]{3,0,2,1:T(8,128)(2,1)S(1)} all-to-all(bf16[8,4,6,1536]{3,0,2,1:T(8,128)(2,1)S(1)} %copy.52), channel_id=1, replica_groups=mesh['dp'=4,'expert'=8,'etp'=8] {'dp'}, dimensions={1} | all-to-all | bytes 1179648 | tf_op jit(solution)/shard_map/all_to_all | solution.py:53
  24.9 0.5 copy.53
  25.4 1.4 broadcast_in_dim.26
  26.8 118.2 %all_to_all.41 = bf16[64,4,6,1536]{3,1,2,0:T(4,128)(2,1)S(1)} all-to-all(bf16[64,4,6,1536]{3,1,2,0:T(4,128)(2,1)S(1)} %bitcast.46), channel_id=1, replica_groups=mesh['dp'=4,'expert'=8,'etp'=8] {'expert','etp'}, dimensions={0} | all-to-all | bytes 9437184 | tf_op jit(solution)/shard_map/all_to_all | solution.py:65
  145.0 4.4 copy.54
  149.4 8.5 %reshape.100 = bf16[1536,1536]{1,0:T(8,128)(2,1)} reshape(bf16[64,4,6,1536]{3,2,1,0:T(8,128)(2,1)} %copy.54) | data formatting | bytes 9437184 | tf_op jit(solution)/shard_map/reshape | solution.py:69
  157.9 9.2 %fusion.16 = f32[1536,768]{1,0:T(8,128)} fusion(bf16[1536,1536]{1,0:T(8,128)(2,1)} %reshape.100, bf16[1,768,1536]{2,1,0:T(8,128)(2,1)} %param.11), kind=kOutput, calls=%fused_computation.22 | convolution fusion | flops 3623878656 | bytes 11796480 | tf_op jit(solution)/shard_map/sq,fq->sf/dot_general | solution.py:74
  167.0 0.0 copy-start.2
  167.0 0.0 all-reduce.2.cloned.1.call-update
  167.1 0.7 copy-done.2
  167.7 0.1 select_reduce_fusion.1
  167.8 0.1 convert_element_type.56
  167.9 7.6 %all_to_all.42 = bf16[8,4,6]{2,0,1:T(8,128)(2,1)S(1)} all-to-all(bf16[8,4,6]{2,0,1:T(8,128)(2,1)S(1)} %broadcast_in_dim.50), channel_id=1, replica_groups=mesh['dp'=4,'expert'=8,'etp'=8] {'dp'}, dimensions={1} | all-to-all | bytes 768 | tf_op jit(solution)/shard_map/all_to_all | solution.py:54
  175.6 15.6 %all_to_all.43 = bf16[64,4,6]{2,1,0:T(4,128)(2,1)S(1)} all-to-all(bf16[64,4,6]{2,1,0:T(4,128)(2,1)S(1)} %bitcast.49), channel_id=1, replica_groups=mesh['dp'=4,'expert'=8,'etp'=8] {'expert','etp'}, dimensions={0} | all-to-all | bytes 6144 | tf_op jit(solution)/shard_map/all_to_all | solution.py:66
  191.2 0.1 reshape.106
  191.4 78.0 %all-reduce.2.cloned.1.call-done = f32[1536,768]{1,0:T(8,128)} async-done(((f32[1536,768]{1,0:T(8,128)}), f32[1536,768]{1,0:T(8,128)}) %all-reduce.2.cloned.1.call-update) | async-done | bytes 4718608 | tf_op jit(solution)/shard_map/psum | solution.py:75
  269.3 0.0 copy-done
  269.4 12.6 %fusion.12 = f32[1536,1536]{1,0:T(8,128)} fusion(bf16[1,1536,768]{2,1,0:T(8,128)(2,1)S(1)} %copy-done, f32[1536,768]{1,0:T(8,128)} %all-reduce.2.cloned.1.call-done, bf16[1,1536,768]{2,1,0:T(8,128)(2,1)} %param.15, bf16[1,1536,768]{2,1,0:T(8,128)(2,1)} %param.14, f32[1536]{0:T(1024)S(1)} %reshape.106), kind=kOutput, calls=%fused_computation.19 | convolution fusion | flops 3639214080 | bytes 21239808 | tf_op jit(solution)/shard_map/sf,qf->sq/dot_general | solution.py:77
  281.9 0.0 copy-done.3
  281.9 0.0 copy-done.4
  281.9 0.0 copy-done.5
  281.9 9.5 %convolution_add_fusion = f32[1536,1536]{1,0:T(8,128)} fusion(f32[1536,1536]{1,0:T(8,128)} %fusion.12, f32[1536,768]{1,0:T(8,128)S(1)} %copy-done.3, bf16[1,1536,768]{2,1,0:T(8,128)(2,1)S(1)} %copy-done.5, bf16[1,1536,768]{2,1,0:T(8,128)(2,1)S(1)} %copy-done.4, f32[1536]{0:T(1024)S(1)} %reshape.106), kind=kOutput, calls=%fused_computation.2 | convolution fusion | flops 3635675136 | bytes 28317696 | tf_op jit(solution)/shard_map/sf,qf->sq/dot_general | solution.py:80
  291.4 11.4 %reshape.102 = f32[64,4,6,1536]{3,2,1,0:T(8,128)} reshape(f32[1536,1536]{1,0:T(8,128)} %convolution_add_fusion) | data formatting | bytes 18874368 | tf_op jit(solution)/shard_map/reshape | solution.py:83
  302.8 17.0 %copy.56 = f32[64,4,6,1536]{3,1,2,0:T(4,128)} copy(f32[64,4,6,1536]{3,2,1,0:T(8,128)} %reshape.102) | data formatting | bytes 18874368 | tf_op jit(solution)/shard_map/reshape | solution.py:83
  319.8 218.2 %all_to_all.44 = f32[64,4,6,1536]{3,1,2,0:T(4,128)S(1)} all-to-all(f32[64,4,6,1536]{3,1,2,0:T(4,128)} %copy.56), channel_id=1, replica_groups=mesh['dp'=4,'expert'=8,'etp'=8] {'expert','etp'}, dimensions={0} | all-to-all | bytes 18874368 | tf_op jit(solution)/shard_map/all_to_all | solution.py:84
  537.9 1.5 bitcast_reduce_fusion
  539.4 1.7 copy.58
  541.1 3.5 all-to-all-start.5
  544.7 0.1 copy.60
  544.8 0.1 reshape.105
  544.8 0.1 copy.50
  544.9 16.9 %all-to-all-done.5 = f32[8,4,6,1536]{3,0,2,1:T(8,128)S(1)} async-done(((f32[8,4,6,1536]{3,0,2,1:T(8,128)}), f32[8,4,6,1536]{3,0,2,1:T(8,128)S(1)}, u32[]{:S(2)}, u32[]{:S(2)}) %all-to-all-start.5) | async-done | bytes 1179680 | tf_op jit(solution)/shard_map/all_to_all | solution.py:88
  561.8 0.8 copy.59
  562.6 0.4 copy.66
  563.0 0.0 copy-start.1
  563.0 1.7 gather_fusion
  564.6 1.4 gather.7
  566.0 1.2 select_reduce_fusion
  567.2 0.0 copy-done.1
  (12 shorter events, 0.1 us)
Async XLA Ops:
  6.5 262.8 %copy-start = (bf16[1,1536,768]{2,1,0:T(8,128)(2,1)S(1)}, bf16[1,1536,768]{2,1,0:T(8,128)(2,1)}, u32[]{:S(2)}) copy-start(bf16[1,1536,768]{2,1,0:T(8,128)(2,1)} %param.12) | copy-start | bytes 7077892
  6.5 262.8 %all-reduce.2.cloned.1.call-start = ((), (), s32[]{:S(2)}) async-start(), calls=%async_computation.6 | async-start | bytes 9437184 | tf_op jit(solution)/shard_map/psum | solution.py:75
  167.0 0.7 copy-start.2
  269.3 12.6 %copy-start.3 = (f32[1536,768]{1,0:T(8,128)S(1)}, f32[1536,768]{1,0:T(8,128)}, u32[]{:S(2)}) copy-start(f32[1536,768]{1,0:T(8,128)} %all-reduce.2.cloned.1.call-done) | copy-start | bytes 14155780
  269.3 12.6 %copy-start.4 = (bf16[1,1536,768]{2,1,0:T(8,128)(2,1)S(1)}, bf16[1,1536,768]{2,1,0:T(8,128)(2,1)}, u32[]{:S(2)}) copy-start(bf16[1,1536,768]{2,1,0:T(8,128)(2,1)} %param.14) | copy-start | bytes 7077892
  269.3 12.6 %copy-start.5 = (bf16[1,1536,768]{2,1,0:T(8,128)(2,1)S(1)}, bf16[1,1536,768]{2,1,0:T(8,128)(2,1)}, u32[]{:S(2)}) copy-start(bf16[1,1536,768]{2,1,0:T(8,128)(2,1)} %param.13) | copy-start | bytes 7077892
  541.1 20.7 %all-to-all-start.5 = ((f32[8,4,6,1536]{3,0,2,1:T(8,128)}), f32[8,4,6,1536]{3,0,2,1:T(8,128)S(1)}, u32[]{:S(2)}, u32[]{:S(2)}) async-start(f32[8,4,6,1536]{3,0,2,1:T(8,128)} %copy.58), calls=%async_computation.5 | async-start | bytes 2359296 | tf_op jit(solution)/shard_map/all_to_all | solution.py:88
  563.0 4.3 copy-start.1
Sparse Core Ops, SparseCore 0:
  167.2 102.1 all-reduce.1
where the time goes:
time: 575 us; the launch traced here: 574 us
  blocking collectives  374 us (65%)
  waiting for transfers between devices  94.9 us (17%)
  local copies, waits for them, and re-layouts  50.4 us (9%)
  matrix products  32.4 us (6%)
  between operations  13.5 us (2%)
    all_to_all x1, blocking collectives, on_device(): lax.all_to_all(outbound, ('expert', 'etp'), split_axis=0, concat_axis=0,...  218 us
    all_to_all x1, blocking collectives, on_device(): lax.all_to_all(copied, ('expert', 'etp'), split_axis=0, concat_axis=0, ti...  118 us
    psum x1, waiting for transfers between devices, on_device(): hidden_raw = lax.psum(partial_value, 'dp')  78 us
    reshape x2, local copies, waits for them, and re-layouts, on_device(): slot_grad.reshape(expert_count * tensor_count, group_count, capacity, qua...  28.4 us
    all_to_all x1, waiting for transfers between devices, on_device(): lax.all_to_all(inbound, 'dp', split_axis=1, concat_axis=3, tiled=True)  16.9 us
    all_to_all x1, blocking collectives, on_device(): lax.all_to_all(copied_weight, ('expert', 'etp'), split_axis=0, concat_axi...  15.6 us
    all_to_all x1, blocking collectives, on_device(): lax.all_to_all(outgoing, 'dp', split_axis=1, concat_axis=1, tiled=True)  14.3 us
    dot_general x1, matrix products, on_device(): jnp.einsum('sf,qf->sq', gate_grad, gate_weight[0], preferred_element_type...  12.6 us
  transfers between devices with their start and end apart: 2, of which 2 were waited for; matrix products, arithmetic and copies ran while one was open for 0% of the time, Pallas kernels for 0%

commit v1 on v0

--- a/solution.py
+++ b/solution.py
@@ -72,7 +72,10 @@
     gate_local = gate_saved[0]
     up_local = up_saved[0]
     partial_value = jnp.einsum("sq,fq->sf", routed, down_local, preferred_element_type=jnp.float32)
-    hidden_raw = lax.psum(partial_value, "dp")
+    count, hidden_raw = (lax.axis_size("dp"), partial_value)
+    for far in [1 << k for k in range(count.bit_length() - 1)]:
+        swap = [(i, i ^ far) for i in range(count)]
+        hidden_raw = hidden_raw + lax.ppermute(hidden_raw, "dp", swap)
     gate_grad, up_grad = swiglu_backward(hidden_raw, slot_weight, gate_local, up_local)
     slot_grad = jnp.einsum(
         "sf,qf->sq", gate_grad, gate_weight[0], preferred_element_type=jnp.float32

time: 575 us -> 686 us (1.19)
  blocking collectives: 374 us -> 465 us
  waiting for transfers between devices: 94.9 us -> 120 us
  between operations: 13.5 us -> 0.15 us
    ppermute x0 -> x2, waiting for transfers between devices: none -> 104 us  [on_device(): hidden_raw = hidden_raw + lax.ppermute(hidden_raw, 'dp', swap)]
    all_to_all x1, blocking collectives: 7.65 us -> 104 us  [on_device(): lax.all_to_all(weight_out, 'dp', split_axis=1, concat_axis=1, tiled=True)]
    psum x1 -> x0, waiting for transfers between devices: 78 us -> none  [on_device(): hidden_raw = lax.psum(partial_value, 'dp')]
  transfers between devices with their start and end apart: 2 -> 3, of which waited for: 2 -> 2; matrix products, arithmetic and copies ran while one was open for 0% -> 0% of each run, Pallas kernels for 0% -> 0%
where the time goes in v1:
time: 686 us; the launch traced here: 685 us
  blocking collectives  465 us (68%)
  waiting for transfers between devices  120 us (17%)
  local copies, waits for them, and re-layouts  49.8 us (7%)
  matrix products  36.6 us (5%)
  other arithmetic  8.17 us (1%)
    all_to_all x1, blocking collectives, on_device(): lax.all_to_all(outbound, ('expert', 'etp'), split_axis=0, concat_axis=0,...  213 us
    all_to_all x1, blocking collectives, on_device(): lax.all_to_all(copied, ('expert', 'etp'), split_axis=0, concat_axis=0, ti...  118 us
    all_to_all x1, blocking collectives, on_device(): lax.all_to_all(weight_out, 'dp', split_axis=1, concat_axis=1, tiled=True)  104 us
    ppermute x2, waiting for transfers between devices, on_device(): hidden_raw = hidden_raw + lax.ppermute(hidden_raw, 'dp', swap)  104 us
    reshape x2, local copies, waits for them, and re-layouts, on_device(): slot_grad.reshape(expert_count * tensor_count, group_count, capacity, qua...  28.4 us
    all_to_all x1, waiting for transfers between devices, on_device(): lax.all_to_all(inbound, 'dp', split_axis=1, concat_axis=3, tiled=True)  16.8 us
    dot_general x1, matrix products, on_device(): jnp.einsum('sf,qf->sq', up_grad, up_weight[0], preferred_element_type=jnp...  14.8 us
    all_to_all x1, blocking collectives, on_device(): lax.all_to_all(copied_weight, ('expert', 'etp'), split_axis=0, concat_axi...  14.6 us
  transfers between devices with their start and end apart: 3, of which 2 were waited for; matrix products, arithmetic and copies ran while one was open for 0% of the time, Pallas kernels for 0%

profile of v1, /device:TPU:32, one launch (start us, length us, event | category | flops | bytes accessed | tf_op | source)
XLA Modules:
  0.0 684.9 jit_solution(17150475184462956700)
XLA Ops:
  0.0 0.0 copy-start
  0.0 0.9 convert_reduce_fusion
  0.9 0.9 select_reduce_fusion.2
  1.8 0.7 compare_and_fusion
  2.5 0.1 fusion.20
  2.6 0.1 reshape.97
  2.7 0.1 copy.61
  2.9 1.2 fusion.9
  4.1 14.3 %all_to_all.40 = bf16[8,4,6,1536]{3,0,2,1:T(8,128)(2,1)S(1)} all-to-all(bf16[8,4,6,1536]{3,0,2,1:T(8,128)(2,1)S(1)} %copy.52), channel_id=1, replica_groups=mesh['dp'=4,'expert'=8,'etp'=8] {'dp'}, dimensions={1} | all-to-all | bytes 1179648 | tf_op jit(solution)/shard_map/all_to_all | solution.py:53
  18.4 0.5 copy.53
  18.8 1.4 broadcast_in_dim.26
  20.2 118.2 %all_to_all.41 = bf16[64,4,6,1536]{3,1,2,0:T(4,128)(2,1)S(1)} all-to-all(bf16[64,4,6,1536]{3,1,2,0:T(4,128)(2,1)S(1)} %bitcast.46), channel_id=1, replica_groups=mesh['dp'=4,'expert'=8,'etp'=8] {'expert','etp'}, dimensions={0} | all-to-all | bytes 9437184 | tf_op jit(solution)/shard_map/all_to_all | solution.py:65
  138.4 4.4 copy.54
  142.9 8.5 %reshape.100 = bf16[1536,1536]{1,0:T(8,128)(2,1)} reshape(bf16[64,4,6,1536]{3,2,1,0:T(8,128)(2,1)} %copy.54) | data formatting | bytes 9437184 | tf_op jit(solution)/shard_map/reshape | solution.py:69
  151.3 6.4 fusion.16
  157.8 0.0 copy-start.2
  157.8 0.6 collective-permute-start
  158.4 103.6 %collective-permute-done = f32[1536,768]{1,0:T(8,128)S(1)} collective-permute-done((f32[1536,768]{1,0:T(8,128)S(1)}, f32[1536,768]{1,0:T(8,128)S(1)}, u32[]{:S(2)}, u32[]{:S(2)}) %collective-permute-start) | collective-permute-done | bytes 4718624 | tf_op jit(solution)/shard_map/ppermute | solution.py:78
  262.0 2.7 add.43
  264.8 1.0 collective-permute-start.1
  265.8 0.0 copy-done.2
  265.8 0.1 select_reduce_fusion.1
  265.9 0.1 convert_element_type.56
  266.0 104.0 %all_to_all.42 = bf16[8,4,6]{2,0,1:T(8,128)(2,1)S(1)} all-to-all(bf16[8,4,6]{2,0,1:T(8,128)(2,1)S(1)} %broadcast_in_dim.50), channel_id=1, replica_groups=mesh['dp'=4,'expert'=8,'etp'=8] {'dp'}, dimensions={1} | all-to-all | bytes 768 | tf_op jit(solution)/shard_map/all_to_all | solution.py:54
  370.0 14.6 %all_to_all.43 = bf16[64,4,6]{2,1,0:T(4,128)(2,1)S(1)} all-to-all(bf16[64,4,6]{2,1,0:T(4,128)(2,1)S(1)} %bitcast.49), channel_id=1, replica_groups=mesh['dp'=4,'expert'=8,'etp'=8] {'expert','etp'}, dimensions={0} | all-to-all | bytes 6144 | tf_op jit(solution)/shard_map/all_to_all | solution.py:66
  384.6 0.1 reshape.106
  384.7 0.0 copy-start.3
  384.8 0.0 copy-start.4
  384.8 0.0 collective-permute-done.1
  384.8 0.0 copy-done
  384.8 14.1 %fusion.12 = f32[1536,1536]{1,0:T(8,128)} fusion(bf16[1,1536,768]{2,1,0:T(8,128)(2,1)S(1)} %copy-done, bf16[1,1536,768]{2,1,0:T(8,128)(2,1)} %param.15, bf16[1,1536,768]{2,1,0:T(8,128)(2,1)} %param.14, f32[1536,768]{1,0:T(8,128)} %add.43, f32[1536,768]{1,0:T(8,128)} %collective-permute-done.1, f32[1536]{0:T(1024)S(1)} %reshape.106), kind=kOutput, calls=%fused_computation.20 | convolution fusion | flops 3640393728 | bytes 25958400 | tf_op jit(solution)/shard_map/sf,qf->sq/dot_general | solution.py:80
  398.9 14.8 %convolution_add_fusion = f32[1536,1536]{1,0:T(8,128)} fusion(f32[1536,1536]{1,0:T(8,128)} %fusion.12, bf16[1,1536,768]{2,1,0:T(8,128)(2,1)S(1)} %copy-done.4, bf16[1,1536,768]{2,1,0:T(8,128)(2,1)S(1)} %copy-done.3, f32[1536,768]{1,0:T(8,128)} %add.43, f32[1536,768]{1,0:T(8,128)} %collective-permute-done.1, f32[1536]{0:T(1024)S(1)} %reshape.106), kind=kOutput, calls=%fused_computation.2 | convolution fusion | flops 3636854784 | bytes 33036288 | tf_op jit(solution)/shard_map/sf,qf->sq/dot_general | solution.py:83
  413.7 11.4 %reshape.102 = f32[64,4,6,1536]{3,2,1,0:T(8,128)} reshape(f32[1536,1536]{1,0:T(8,128)} %convolution_add_fusion) | data formatting | bytes 18874368 | tf_op jit(solution)/shard_map/reshape | solution.py:86
  425.1 17.0 %copy.56 = f32[64,4,6,1536]{3,1,2,0:T(4,128)} copy(f32[64,4,6,1536]{3,2,1,0:T(8,128)} %reshape.102) | data formatting | bytes 18874368 | tf_op jit(solution)/shard_map/reshape | solution.py:86
  442.1 213.5 %all_to_all.44 = f32[64,4,6,1536]{3,1,2,0:T(4,128)S(1)} all-to-all(f32[64,4,6,1536]{3,1,2,0:T(4,128)} %copy.56), channel_id=1, replica_groups=mesh['dp'=4,'expert'=8,'etp'=8] {'expert','etp'}, dimensions={0} | all-to-all | bytes 18874368 | tf_op jit(solution)/shard_map/all_to_all | solution.py:87
  655.6 1.5 bitcast_reduce_fusion
  657.1 1.7 copy.58
  658.8 3.5 all-to-all-start.5
  662.3 0.1 copy.60
  662.4 0.1 reshape.105
  662.5 0.1 copy.50
  662.6 16.8 %all-to-all-done.5 = f32[8,4,6,1536]{3,0,2,1:T(8,128)S(1)} async-done(((f32[8,4,6,1536]{3,0,2,1:T(8,128)}), f32[8,4,6,1536]{3,0,2,1:T(8,128)S(1)}, u32[]{:S(2)}, u32[]{:S(2)}) %all-to-all-start.5) | async-done | bytes 1179680 | tf_op jit(solution)/shard_map/all_to_all | solution.py:91
  679.4 0.8 copy.59
  680.2 0.4 copy.66
  680.6 0.0 copy-start.1
  680.6 1.7 gather_fusion
  682.3 1.4 gather.7
  683.6 1.2 select_reduce_fusion
  (12 shorter events, 0.1 us)
Async XLA Ops:
  0.0 384.8 %copy-start = (bf16[1,1536,768]{2,1,0:T(8,128)(2,1)S(1)}, bf16[1,1536,768]{2,1,0:T(8,128)(2,1)}, u32[]{:S(2)}) copy-start(bf16[1,1536,768]{2,1,0:T(8,128)(2,1)} %param.12) | copy-start | bytes 7077892
  157.8 108.0 %copy-start.2 = (bf16[8,4]{0,1:T(4,128)(2,1)S(1)}, bf16[8,4]{0,1:T(4,128)(2,1)}, u32[]{:S(2)}) copy-start(bf16[8,4]{0,1:T(4,128)(2,1)} %param.9) | copy-start | bytes 196
  157.8 104.2 %collective-permute-start = (f32[1536,768]{1,0:T(8,128)S(1)}, f32[1536,768]{1,0:T(8,128)S(1)}, u32[]{:S(2)}, u32[]{:S(2)}) collective-permute-start(f32[1536,768]{1,0:T(8,128)S(1)} %fusion.16), channel_id=1, source_target_pairs={{0,64},{64,0},{128,192},{192,128},{1,65},{65,1},{129,193},{193,129... | collective-permute-start | bytes 14155784 | tf_op jit(solution)/shard_map/ppermute | solution.py:78
  264.8 120.0 %collective-permute-start.1 = (f32[1536,768]{1,0:T(8,128)}, f32[1536,768]{1,0:T(8,128)}, u32[]{:S(2)}, u32[]{:S(2)}) collective-permute-start(f32[1536,768]{1,0:T(8,128)} %add.43), channel_id=1, source_target_pairs={{0,128},{64,192},{128,0},{192,64},{1,129},{65,193},{129,1},{193,65... | collective-permute-start | bytes 14155784 | tf_op jit(solution)/shard_map/ppermute | solution.py:78
  384.7 14.2 %copy-start.3 = (bf16[1,1536,768]{2,1,0:T(8,128)(2,1)S(1)}, bf16[1,1536,768]{2,1,0:T(8,128)(2,1)}, u32[]{:S(2)}) copy-start(bf16[1,1536,768]{2,1,0:T(8,128)(2,1)} %param.14) | copy-start | bytes 7077892
  384.8 14.2 %copy-start.4 = (bf16[1,1536,768]{2,1,0:T(8,128)(2,1)S(1)}, bf16[1,1536,768]{2,1,0:T(8,128)(2,1)}, u32[]{:S(2)}) copy-start(bf16[1,1536,768]{2,1,0:T(8,128)(2,1)} %param.13) | copy-start | bytes 7077892
  658.8 20.6 %all-to-all-start.5 = ((f32[8,4,6,1536]{3,0,2,1:T(8,128)}), f32[8,4,6,1536]{3,0,2,1:T(8,128)S(1)}, u32[]{:S(2)}, u32[]{:S(2)}) async-start(f32[8,4,6,1536]{3,0,2,1:T(8,128)} %copy.58), calls=%async_computation.5 | async-start | bytes 2359296 | tf_op jit(solution)/shard_map/all_to_all | solution.py:91
  680.6 4.3 copy-start.1
